TPU v7x, 32 devices: a whole 2x2x4 slice. The times are simulated.
32 devices in a mesh: dp: 16 (over z, x, core), fsdp: 2 (over y).
Axes of the slice: x: 2, y: 2, z: 4, core: 2. Of those that a mesh axis runs over, the one named last changes fastest.
Arguments:
- tokens: bfloat16 [32, 512, 768], P(('dp', 'fsdp')), may hold values from -6 to 6
- context: bfloat16 [32, 1024, 768], P(('dp', 'fsdp')), may hold values from -6 to 6
- past_coeffs: bfloat16 [32, 512, 768], P(('dp', 'fsdp')), may hold values from -6 to 6
- doc_lengths: int32 [32, 4], P(('dp', 'fsdp')), may hold values from 1 to 256, 512 in all within a row
- carried: int32 [32], P(('dp', 'fsdp')), may hold values 0 or 1
- histogram: int32 [32, 64], P(('dp', 'fsdp')), may hold values from 1 to 128, 512 in all within a row
- cotangent: bfloat16 [32, 512, 768], P(('dp', 'fsdp')), may hold values from -6 to 6
- attn_gain: bfloat16 [768], P(('dp', 'fsdp')), may hold values from 0.5 to 1.5
- attn_shift: bfloat16 [768], P(('dp', 'fsdp')), may hold values from -2 to 2
- project_in: bfloat16 [768, 2304], P('dp', 'fsdp'), may hold values from -0.21875 to 0.21875
- query_bias: bfloat16 [768], P(('dp', 'fsdp')), may hold values from -2 to 2
- value_bias: bfloat16 [768], P(('dp', 'fsdp')), may hold values from -2 to 2
- project_out: bfloat16 [768, 768], P('dp', 'fsdp'), may hold values from -0.625 to 0.625
- out_bias: bfloat16 [768], P(('dp', 'fsdp')), may hold values from -2 to 2
- memory_keys: bfloat16 [768, 768], P('dp', 'fsdp'), may hold values from -0.21875 to 0.21875
- memory_values: bfloat16 [768, 768], P('dp', 'fsdp'), may hold values from -0.4375 to 0.4375
- centre_weight: bfloat16 [512, 12], P(('dp', 'fsdp')), may hold values from -0.25 to 0.25
- spread_weight: bfloat16 [512, 12], P(('dp', 'fsdp')), may hold values from -0.25 to 0.25
- mlp_gain: bfloat16 [768], P(('dp', 'fsdp')), may hold values from 0.5 to 1.5
- mlp_shift: bfloat16 [768], P(('dp', 'fsdp')), may hold values from -2 to 2
- up_weight: bfloat16 [768, 3072], P('dp', 'fsdp'), may hold values from -0.21875 to 0.21875
- up_bias: bfloat16 [3072], P(('dp', 'fsdp')), may hold values from -2 to 2
- down_weight: bfloat16 [3072, 768], P('dp', 'fsdp'), may hold values from -0.109375 to 0.109375
- down_bias: bfloat16 [768], P(('dp', 'fsdp')), may hold values from -2 to 2
Outputs:
- output: bfloat16 [32, 512, 768], P(('dp', 'fsdp'))
- grad_tokens: float32 [32, 512, 768], P(('dp', 'fsdp'))
- grad_attn_gain: float32 [768], P(('dp', 'fsdp'))
- grad_attn_shift: float32 [768], P(('dp', 'fsdp'))
- grad_project_in: float32 [768, 2304], P('dp', 'fsdp')
- grad_query_bias: float32 [768], P(('dp', 'fsdp'))
- grad_value_bias: float32 [768], P(('dp', 'fsdp'))
- grad_project_out: float32 [768, 768], P('dp', 'fsdp')
- grad_out_bias: float32 [768], P(('dp', 'fsdp'))
- grad_memory_keys: float32 [768, 768], P('dp', 'fsdp')
- grad_memory_values: float32 [768, 768], P('dp', 'fsdp')
- grad_centre_weight: float32 [512, 12], P(('dp', 'fsdp'))
- grad_spread_weight: float32 [512, 12], P(('dp', 'fsdp'))
- grad_mlp_gain: float32 [768], P(('dp', 'fsdp'))
- grad_mlp_shift: float32 [768], P(('dp', 'fsdp'))
- grad_up_weight: float32 [768, 3072], P('dp', 'fsdp')
- grad_up_bias: float32 [3072], P(('dp', 'fsdp'))
- grad_down_weight: float32 [3072, 768], P('dp', 'fsdp')
- grad_down_bias: float32 [768], P(('dp', 'fsdp'))
- locations: float32 [32, 512], P(('dp', 'fsdp'))
Inputs may be any that keep to these rules, and one draw needn't show every extreme that they name: `doc_lengths`: the 4 document lengths of a segment, in order, sum to 512. `histogram`: A segment's 64 bin counts sum to 512.
All inputs are finite; a program needn't handle non-finite values. No bound on the sum of `carried` on one device may be relied on, other than what follows from the above.
Results may differ from a plain program's by a relative error of at most 0.025.
Values may be sent and summed in bfloat16 or wider, within the bound.
No kernel may reach another device: no remote copies, remote signals or barrier semaphores. Data moves between devices by JAX's collectives and lax.ppermute only.
A program may use at most 192 MiB of HBM per device.

v0:
```python
import jax
import jax.numpy as jnp
from jax import lax
from jax.sharding import PartitionSpec as P

H = 12
DH = 64
N = 512
CTX = 1024
M = 512
NBINS = 64


precise = lax.Precision.HIGHEST
memory_tau = 0.75
ridge_weight = 1.0
norm_epsilon = 1e-05
spread_scale = 0.25
masked_fill = -1e30


def for_sending(value):

    def short(part):
        return part.astype(jnp.bfloat16) if part.dtype == jnp.float32 else part

    return jax.tree.map(short, value)


def layer_norm(values, norm_gain, norm_shift):
    row_mean = jnp.mean(values, axis=-1, keepdims=True)
    centred = values - row_mean
    variance = jnp.mean(centred * centred, axis=-1, keepdims=True)
    return centred * lax.rsqrt(variance + norm_epsilon) * norm_gain + norm_shift


def gelu_tanh(values):
    return jax.nn.gelu(values, approximate=True)


def basis_table(points):
    centres = (jnp.arange(N, dtype=jnp.float32) + 0.5) / N
    distance = points[:, None] - centres[None, :]
    return jnp.exp(-0.5 * distance * distance * (N * N))


def sample_points(histogram):
    bin_ends = jnp.cumsum(histogram)
    bin_starts = bin_ends - histogram
    sample_slots = jnp.arange(M, dtype=jnp.int32)
    inside = (
        (sample_slots[:, None] >= bin_starts[None, :]) & (sample_slots[:, None] < bin_ends[None, :])
    ).astype(jnp.int32)
    bin_first = jnp.sum(inside * bin_starts[None, :], axis=1)
    bin_count = jnp.sum(inside * histogram[None, :], axis=1)
    bin_number = jnp.sum(inside * jnp.arange(NBINS, dtype=jnp.int32)[None, :], axis=1)
    offset = (sample_slots - bin_first).astype(jnp.float32) + 0.5
    return (bin_number.astype(jnp.float32) + offset / bin_count.astype(jnp.float32)) / NBINS


def memory_coeffs(context_rows, past_rows, points):
    past_values = jnp.dot(basis_table(points), past_rows.astype(jnp.float32), precision=precise)
    recent = memory_tau + (1.0 - memory_tau) * (jnp.arange(CTX, dtype=jnp.float32) + 0.5) / CTX
    positions = jnp.concatenate([memory_tau * points, recent])
    design = basis_table(positions)
    gram_matrix = jnp.dot(design.T, design, precision=precise) + ridge_weight * jnp.eye(
        N, dtype=jnp.float32
    )
    stacked = jnp.concatenate([past_values, context_rows.astype(jnp.float32)], axis=0)
    right_side = jnp.dot(design.T, stacked, precision=precise)
    factor = jnp.linalg.cholesky(gram_matrix)
    return jax.scipy.linalg.cho_solve((factor, True), right_side)


def read_local(memory_scores, centre_weight, spread_weight):
    centres = (jnp.arange(N, dtype=jnp.float32) + 0.5) / N
    centre = jax.nn.sigmoid(
        jnp.einsum("shn,nh->sh", memory_scores, centre_weight, precision=precise)
    )
    spread = spread_scale * jax.nn.softplus(
        jnp.einsum("shn,nh->sh", memory_scores, spread_weight, precision=precise)
    )
    variance = 1.0 / (N * N) + spread * spread
    distance = centre[..., None] - centres
    return (
        lax.rsqrt(variance)[..., None]
        / N
        * jnp.exp(-0.5 * distance * distance / variance[..., None])
    )


def doc_masks(lengths, carry_flag, seg_rows):
    doc_ends = jnp.cumsum(lengths)
    places = jnp.arange(seg_rows, dtype=jnp.int32)
    document = jnp.sum((places[:, None] >= doc_ends[None, :]).astype(jnp.int32), axis=1)
    allowed = (places[:, None] >= places[None, :]) & (document[:, None] == document[None, :])
    reading = (document == 0).astype(jnp.int32) * carry_flag
    return (allowed, reading.astype(jnp.float32))


def collect_first(shards):
    within = (
        lax.all_gather(shards[0], "fsdp", axis=0, tiled=True),
        lax.all_gather(shards[1], "fsdp", axis=0, tiled=True),
        lax.all_gather(shards[2], "fsdp", axis=1, tiled=True),
        lax.all_gather(shards[3], "fsdp", axis=0, tiled=True),
        lax.all_gather(shards[4], "fsdp", axis=0, tiled=True),
        lax.all_gather(shards[5], "fsdp", axis=1, tiled=True),
        lax.all_gather(shards[6], "fsdp", axis=0, tiled=True),
        lax.all_gather(shards[7], "fsdp", axis=1, tiled=True),
        lax.all_gather(shards[8], "fsdp", axis=1, tiled=True),
        lax.all_gather(shards[9], "fsdp", axis=0, tiled=True),
        lax.all_gather(shards[10], "fsdp", axis=0, tiled=True),
        lax.all_gather(shards[11], "fsdp", axis=0, tiled=True),
        lax.all_gather(shards[12], "fsdp", axis=0, tiled=True),
        lax.all_gather(shards[13], "fsdp", axis=1, tiled=True),
        lax.all_gather(shards[14], "fsdp", axis=0, tiled=True),
        lax.all_gather(shards[15], "fsdp", axis=1, tiled=True),
        lax.all_gather(shards[16], "fsdp", axis=0, tiled=True),
    )
    return (
        lax.all_gather(within[0], "dp", axis=0, tiled=True),
        lax.all_gather(within[1], "dp", axis=0, tiled=True),
        lax.all_gather(within[2], "dp", axis=0, tiled=True),
        lax.all_gather(within[3], "dp", axis=0, tiled=True),
        lax.all_gather(within[4], "dp", axis=0, tiled=True),
        lax.all_gather(within[5], "dp", axis=0, tiled=True),
        lax.all_gather(within[6], "dp", axis=0, tiled=True),
        lax.all_gather(within[7], "dp", axis=0, tiled=True),
        lax.all_gather(within[8], "dp", axis=0, tiled=True),
        lax.all_gather(within[9], "dp", axis=0, tiled=True),
        lax.all_gather(within[10], "dp", axis=0, tiled=True),
        lax.all_gather(within[11], "dp", axis=0, tiled=True),
        lax.all_gather(within[12], "dp", axis=0, tiled=True),
        lax.all_gather(within[13], "dp", axis=0, tiled=True),
        lax.all_gather(within[14], "dp", axis=0, tiled=True),
        lax.all_gather(within[15], "dp", axis=0, tiled=True),
        lax.all_gather(within[16], "dp", axis=0, tiled=True),
    )


def collect_again(shards):
    within = (
        lax.all_gather(shards[0], "fsdp", axis=0, tiled=True),
        lax.all_gather(shards[1], "fsdp", axis=0, tiled=True),
        lax.all_gather(shards[2], "fsdp", axis=1, tiled=True),
        lax.all_gather(shards[3], "fsdp", axis=0, tiled=True),
        lax.all_gather(shards[4], "fsdp", axis=0, tiled=True),
        lax.all_gather(shards[5], "fsdp", axis=1, tiled=True),
        lax.all_gather(shards[6], "fsdp", axis=0, tiled=True),
        lax.all_gather(shards[7], "fsdp", axis=1, tiled=True),
        lax.all_gather(shards[8], "fsdp", axis=1, tiled=True),
        lax.all_gather(shards[9], "fsdp", axis=0, tiled=True),
        lax.all_gather(shards[10], "fsdp", axis=0, tiled=True),
        lax.all_gather(shards[11], "fsdp", axis=0, tiled=True),
        lax.all_gather(shards[12], "fsdp", axis=0, tiled=True),
        lax.all_gather(shards[13], "fsdp", axis=1, tiled=True),
        lax.all_gather(shards[14], "fsdp", axis=0, tiled=True),
        lax.all_gather(shards[15], "fsdp", axis=1, tiled=True),
        lax.all_gather(shards[16], "fsdp", axis=0, tiled=True),
    )
    return (
        lax.all_gather(within[0], "dp", axis=0, tiled=True),
        lax.all_gather(within[1], "dp", axis=0, tiled=True),
        lax.all_gather(within[2], "dp", axis=0, tiled=True),
        lax.all_gather(within[3], "dp", axis=0, tiled=True),
        lax.all_gather(within[4], "dp", axis=0, tiled=True),
        lax.all_gather(within[5], "dp", axis=0, tiled=True),
        lax.all_gather(within[6], "dp", axis=0, tiled=True),
        lax.all_gather(within[7], "dp", axis=0, tiled=True),
        lax.all_gather(within[8], "dp", axis=0, tiled=True),
        lax.all_gather(within[9], "dp", axis=0, tiled=True),
        lax.all_gather(within[10], "dp", axis=0, tiled=True),
        lax.all_gather(within[11], "dp", axis=0, tiled=True),
        lax.all_gather(within[12], "dp", axis=0, tiled=True),
        lax.all_gather(within[13], "dp", axis=0, tiled=True),
        lax.all_gather(within[14], "dp", axis=0, tiled=True),
        lax.all_gather(within[15], "dp", axis=0, tiled=True),
        lax.all_gather(within[16], "dp", axis=0, tiled=True),
    )


def spread_grads(totals):
    partial_sums = jax.tree.map(
        lambda part: part.astype(jnp.float32),
        lax.psum_scatter(for_sending(totals), "dp", scatter_dimension=0, tiled=True),
    )
    return (
        lax.psum_scatter(
            partial_sums[0].astype(jnp.bfloat16), "fsdp", scatter_dimension=0, tiled=True
        ).astype(jnp.float32),
        lax.psum_scatter(
            partial_sums[1].astype(jnp.bfloat16), "fsdp", scatter_dimension=0, tiled=True
        ).astype(jnp.float32),
        lax.psum_scatter(
            partial_sums[2].astype(jnp.bfloat16), "fsdp", scatter_dimension=1, tiled=True
        ).astype(jnp.float32),
        lax.psum_scatter(
            partial_sums[3].astype(jnp.bfloat16), "fsdp", scatter_dimension=0, tiled=True
        ).astype(jnp.float32),
        lax.psum_scatter(
            partial_sums[4].astype(jnp.bfloat16), "fsdp", scatter_dimension=0, tiled=True
        ).astype(jnp.float32),
        lax.psum_scatter(
            partial_sums[5].astype(jnp.bfloat16), "fsdp", scatter_dimension=1, tiled=True
        ).astype(jnp.float32),
        lax.psum_scatter(
            partial_sums[6].astype(jnp.bfloat16), "fsdp", scatter_dimension=0, tiled=True
        ).astype(jnp.float32),
        lax.psum_scatter(
            partial_sums[7].astype(jnp.bfloat16), "fsdp", scatter_dimension=1, tiled=True
        ).astype(jnp.float32),
        lax.psum_scatter(
            partial_sums[8].astype(jnp.bfloat16), "fsdp", scatter_dimension=1, tiled=True
        ).astype(jnp.float32),
        lax.psum_scatter(
            partial_sums[9].astype(jnp.bfloat16), "fsdp", scatter_dimension=0, tiled=True
        ).astype(jnp.float32),
        lax.psum_scatter(
            partial_sums[10].astype(jnp.bfloat16), "fsdp", scatter_dimension=0, tiled=True
        ).astype(jnp.float32),
        lax.psum_scatter(
            partial_sums[11].astype(jnp.bfloat16), "fsdp", scatter_dimension=0, tiled=True
        ).astype(jnp.float32),
        lax.psum_scatter(
            partial_sums[12].astype(jnp.bfloat16), "fsdp", scatter_dimension=0, tiled=True
        ).astype(jnp.float32),
        lax.psum_scatter(
            partial_sums[13].astype(jnp.bfloat16), "fsdp", scatter_dimension=1, tiled=True
        ).astype(jnp.float32),
        lax.psum_scatter(
            partial_sums[14].astype(jnp.bfloat16), "fsdp", scatter_dimension=0, tiled=True
        ).astype(jnp.float32),
        lax.psum_scatter(
            partial_sums[15].astype(jnp.bfloat16), "fsdp", scatter_dimension=1, tiled=True
        ).astype(jnp.float32),
        lax.psum_scatter(
            partial_sums[16].astype(jnp.bfloat16), "fsdp", scatter_dimension=0, tiled=True
        ).astype(jnp.float32),
    )


def short_scores(queries, key_rows, allowed):
    raw_scores = jnp.einsum(
        "shd,thd->hst", queries, key_rows, preferred_element_type=jnp.float32
    ) * DH ** (-0.5)
    return jnp.where(allowed[None], raw_scores, masked_fill)


def forward_segment(tokens_seg, coeff_low, allowed, reading, weights):
    (
        attn_gain,
        attn_shift,
        project_in,
        query_bias,
        value_bias,
        project_out,
        out_bias,
        memory_keys,
        memory_values,
        centre_weight,
        spread_weight,
        mlp_gain,
        mlp_shift,
        up_weight,
        up_bias,
        down_weight,
        down_bias,
    ) = weights
    seg_rows = tokens_seg.shape[0]
    model_width = H * DH
    score_scale = DH ** (-0.5)
    inputs = tokens_seg.astype(jnp.float32)
    normed = layer_norm(
        inputs, attn_gain.astype(jnp.float32), attn_shift.astype(jnp.float32)
    ).astype(jnp.bfloat16)
    in_bias = jnp.concatenate([query_bias, jnp.zeros_like(query_bias), value_bias]).astype(
        jnp.float32
    )
    projected = (jnp.dot(normed, project_in, preferred_element_type=jnp.float32) + in_bias).astype(
        jnp.bfloat16
    )
    queries = projected[:, :model_width].reshape(seg_rows, H, DH)
    key_rows = projected[:, model_width : 2 * model_width].reshape(seg_rows, H, DH)
    values = projected[:, 2 * model_width :].reshape(seg_rows, H, DH)
    scores = short_scores(queries, key_rows, allowed)
    log_total = jax.nn.logsumexp(scores, axis=-1, keepdims=True)
    probs_low = jnp.exp(scores - log_total).astype(jnp.bfloat16)
    short_term = jnp.einsum("hst,thd->shd", probs_low, values, preferred_element_type=jnp.float32)
    basis_rows = coeff_low.shape[0]
    memory_key_rows = (
        jnp.dot(coeff_low, memory_keys, preferred_element_type=jnp.float32)
        .astype(jnp.bfloat16)
        .reshape(basis_rows, H, DH)
    )
    memory_value_rows = (
        jnp.dot(coeff_low, memory_values, preferred_element_type=jnp.float32)
        .astype(jnp.bfloat16)
        .reshape(basis_rows, H, DH)
    )
    memory_scores = (
        jnp.einsum("shd,nhd->shn", queries, memory_key_rows, preferred_element_type=jnp.float32)
        * score_scale
    )
    density = read_local(
        memory_scores, centre_weight.astype(jnp.float32), spread_weight.astype(jnp.float32)
    ).astype(jnp.bfloat16)
    recall = jnp.einsum(
        "shn,nhd->shd", density, memory_value_rows, preferred_element_type=jnp.float32
    )
    head_outputs = (
        (short_term + recall * reading[:, None, None])
        .astype(jnp.bfloat16)
        .reshape(seg_rows, model_width)
    )
    middle = (
        inputs
        + jnp.dot(head_outputs, project_out, preferred_element_type=jnp.float32)
        + out_bias.astype(jnp.float32)
    )
    normed_mlp = layer_norm(
        middle, mlp_gain.astype(jnp.float32), mlp_shift.astype(jnp.float32)
    ).astype(jnp.bfloat16)
    hidden = jnp.dot(normed_mlp, up_weight, preferred_element_type=jnp.float32) + up_bias.astype(
        jnp.float32
    )
    active = gelu_tanh(hidden).astype(jnp.bfloat16)
    result = (
        middle
        + jnp.dot(active, down_weight, preferred_element_type=jnp.float32)
        + down_bias.astype(jnp.float32)
    )
    kept_state = (
        inputs,
        normed,
        projected,
        log_total,
        memory_key_rows,
        memory_value_rows,
        memory_scores,
        density,
        head_outputs,
        middle,
        normed_mlp,
        hidden,
        active,
    )
    return (result, kept_state)


def backward_segment(cot_values, coeff_low, allowed, reading, kept_state, weights):
    (
        attn_gain,
        attn_shift,
        project_in,
        query_bias,
        value_bias,
        project_out,
        out_bias,
        memory_keys,
        memory_values,
        centre_weight,
        spread_weight,
        mlp_gain,
        mlp_shift,
        up_weight,
        up_bias,
        down_weight,
        down_bias,
    ) = weights
    (
        inputs,
        normed,
        projected,
        log_total,
        memory_key_rows,
        memory_value_rows,
        memory_scores,
        density,
        head_outputs,
        middle,
        normed_mlp,
        hidden,
        active,
    ) = kept_state
    seg_rows = cot_values.shape[0]
    basis_rows = coeff_low.shape[0]
    model_width = H * DH
    score_scale = DH ** (-0.5)
    queries = projected[:, :model_width].reshape(seg_rows, H, DH)
    key_rows = projected[:, model_width : 2 * model_width].reshape(seg_rows, H, DH)
    values = projected[:, 2 * model_width :].reshape(seg_rows, H, DH)
    cot_float = cot_values.astype(jnp.float32)
    grad_down_bias = jnp.sum(cot_float, axis=0)
    grad_down_weight = jnp.einsum(
        "sf,sd->fd", active, cot_values, preferred_element_type=jnp.float32
    )
    grad_active = jnp.einsum(
        "sd,fd->sf", cot_values, down_weight, preferred_element_type=jnp.float32
    )
    gelu_back = jax.vjp(gelu_tanh, hidden)[1]
    grad_hidden = gelu_back(grad_active)[0].astype(jnp.bfloat16)
    grad_up_bias = jnp.sum(grad_hidden.astype(jnp.float32), axis=0)
    grad_up_weight = jnp.einsum(
        "sd,sf->df", normed_mlp, grad_hidden, preferred_element_type=jnp.float32
    )
    grad_normed_mlp = jnp.einsum(
        "sf,df->sd", grad_hidden, up_weight, preferred_element_type=jnp.float32
    )
    mlp_back = jax.vjp(
        layer_norm, middle, mlp_gain.astype(jnp.float32), mlp_shift.astype(jnp.float32)
    )[1]
    grad_middle_part, grad_mlp_gain, grad_mlp_shift = mlp_back(grad_normed_mlp)
    grad_middle = cot_float + grad_middle_part
    grad_attended = grad_middle.astype(jnp.bfloat16)
    grad_out_bias = jnp.sum(grad_attended.astype(jnp.float32), axis=0)
    grad_project_out = jnp.einsum(
        "se,sd->ed", head_outputs, grad_attended, preferred_element_type=jnp.float32
    )
    grad_heads = jnp.einsum(
        "sd,ed->se", grad_attended, project_out, preferred_element_type=jnp.float32
    )
    grad_heads = grad_heads.astype(jnp.bfloat16).reshape(seg_rows, H, DH)
    scores = short_scores(queries, key_rows, allowed)
    attn_probs = jnp.exp(scores - log_total)
    grad_probs = jnp.einsum("shd,thd->hst", grad_heads, values, preferred_element_type=jnp.float32)
    grad_values = jnp.einsum(
        "hst,shd->thd",
        attn_probs.astype(jnp.bfloat16),
        grad_heads,
        preferred_element_type=jnp.float32,
    )
    row_terms = jnp.sum(attn_probs * grad_probs, axis=-1, keepdims=True)
    grad_scores = (attn_probs * (grad_probs - row_terms)).astype(jnp.bfloat16)
    grad_queries = (
        jnp.einsum("hst,thd->shd", grad_scores, key_rows, preferred_element_type=jnp.float32)
        * score_scale
    )
    grad_keys = (
        jnp.einsum("hst,shd->thd", grad_scores, queries, preferred_element_type=jnp.float32)
        * score_scale
    )
    grad_recall = (grad_heads.astype(jnp.float32) * reading[:, None, None]).astype(jnp.bfloat16)
    grad_density = jnp.einsum(
        "shd,nhd->shn", grad_recall, memory_value_rows, preferred_element_type=jnp.float32
    )
    grad_mem_values = jnp.einsum(
        "shn,shd->nhd", density, grad_recall, preferred_element_type=jnp.float32
    )
    grad_mem_values = grad_mem_values.astype(jnp.bfloat16).reshape(basis_rows, model_width)
    read_back = jax.vjp(
        read_local,
        memory_scores,
        centre_weight.astype(jnp.float32),
        spread_weight.astype(jnp.float32),
    )[1]
    grad_mscores, grad_centre_weight, grad_spread_weight = read_back(grad_density)
    grad_mscores = grad_mscores.astype(jnp.bfloat16)
    grad_queries = (
        grad_queries
        + jnp.einsum(
            "shn,nhd->shd", grad_mscores, memory_key_rows, preferred_element_type=jnp.float32
        )
        * score_scale
    )
    grad_mem_keys = (
        jnp.einsum("shn,shd->nhd", grad_mscores, queries, preferred_element_type=jnp.float32)
        * score_scale
    )
    grad_mem_keys = grad_mem_keys.astype(jnp.bfloat16).reshape(basis_rows, model_width)
    grad_memory_keys = jnp.einsum(
        "nd,ne->de", coeff_low, grad_mem_keys, preferred_element_type=jnp.float32
    )
    grad_memory_values = jnp.einsum(
        "nd,ne->de", coeff_low, grad_mem_values, preferred_element_type=jnp.float32
    )
    grad_projected = jnp.concatenate(
        [
            grad_queries.reshape(seg_rows, model_width),
            grad_keys.reshape(seg_rows, model_width),
            grad_values.reshape(seg_rows, model_width),
        ],
        axis=1,
    ).astype(jnp.bfloat16)
    grad_columns = jnp.sum(grad_projected.astype(jnp.float32), axis=0)
    grad_query_bias = grad_columns[:model_width]
    grad_value_bias = grad_columns[2 * model_width :]
    grad_project_in = jnp.einsum(
        "sd,se->de", normed, grad_projected, preferred_element_type=jnp.float32
    )
    grad_normed = jnp.einsum(
        "se,de->sd", grad_projected, project_in, preferred_element_type=jnp.float32
    )
    attn_back = jax.vjp(
        layer_norm, inputs, attn_gain.astype(jnp.float32), attn_shift.astype(jnp.float32)
    )[1]
    grad_inputs_part, grad_attn_gain, grad_attn_shift = attn_back(grad_normed)
    grad_inputs = grad_middle + grad_inputs_part
    grads = (
        grad_attn_gain,
        grad_attn_shift,
        grad_project_in,
        grad_query_bias,
        grad_value_bias,
        grad_project_out,
        grad_out_bias,
        grad_memory_keys,
        grad_memory_values,
        grad_centre_weight,
        grad_spread_weight,
        grad_mlp_gain,
        grad_mlp_shift,
        grad_up_weight,
        grad_up_bias,
        grad_down_weight,
        grad_down_bias,
    )
    return (grad_inputs, grads)


def local(
    tokens,
    context,
    past_coeffs,
    doc_lengths,
    carried,
    histogram,
    cotangent,
    attn_gain,
    attn_shift,
    project_in,
    query_bias,
    value_bias,
    project_out,
    out_bias,
    memory_keys,
    memory_values,
    centre_weight,
    spread_weight,
    mlp_gain,
    mlp_shift,
    up_weight,
    up_bias,
    down_weight,
    down_bias,
):
    shards = (
        attn_gain,
        attn_shift,
        project_in,
        query_bias,
        value_bias,
        project_out,
        out_bias,
        memory_keys,
        memory_values,
        centre_weight,
        spread_weight,
        mlp_gain,
        mlp_shift,
        up_weight,
        up_bias,
        down_weight,
        down_bias,
    )
    weights = collect_first(shards)
    points = jax.vmap(sample_points)(histogram)
    seg_rows = tokens.shape[1]
    segment_index = 0
    coeff_low = memory_coeffs(
        context[segment_index], past_coeffs[segment_index], points[segment_index]
    ).astype(jnp.bfloat16)
    allowed, reading = doc_masks(doc_lengths[segment_index], carried[segment_index], seg_rows)
    result, kept_state = forward_segment(
        tokens[segment_index], coeff_low, allowed, reading, weights
    )
    results = [result.astype(jnp.bfloat16)]
    states = [kept_state]
    settings = [(coeff_low, allowed, reading)]
    back_weights = collect_again(shards)
    segment_index = 0
    coeff_low, allowed, reading = settings[segment_index]
    grad_inputs, grads = backward_segment(
        cotangent[segment_index], coeff_low, allowed, reading, states[segment_index], back_weights
    )
    input_grads = [grad_inputs]
    (
        grad_attn_gain,
        grad_attn_shift,
        grad_project_in,
        grad_query_bias,
        grad_value_bias,
        grad_project_out,
        grad_out_bias,
        grad_memory_keys,
        grad_memory_values,
        grad_centre_weight,
        grad_spread_weight,
        grad_mlp_gain,
        grad_mlp_shift,
        grad_up_weight,
        grad_up_bias,
        grad_down_weight,
        grad_down_bias,
    ) = spread_grads(grads)
    return (
        jnp.stack(results),
        jnp.stack(input_grads),
        grad_attn_gain,
        grad_attn_shift,
        grad_project_in,
        grad_query_bias,
        grad_value_bias,
        grad_project_out,
        grad_out_bias,
        grad_memory_keys,
        grad_memory_values,
        grad_centre_weight,
        grad_spread_weight,
        grad_mlp_gain,
        grad_mlp_shift,
        grad_up_weight,
        grad_up_bias,
        grad_down_weight,
        grad_down_bias,
        points,
    )


def solution(mesh):
    in_specs = (
        P(("dp", "fsdp"), None, None),
        P(("dp", "fsdp"), None, None),
        P(("dp", "fsdp"), None, None),
        P(("dp", "fsdp"), None),
        P(("dp", "fsdp")),
        P(("dp", "fsdp"), None),
        P(("dp", "fsdp"), None, None),
        P(("dp", "fsdp")),
        P(("dp", "fsdp")),
        P("dp", "fsdp"),
        P(("dp", "fsdp")),
        P(("dp", "fsdp")),
        P("dp", "fsdp"),
        P(("dp", "fsdp")),
        P("dp", "fsdp"),
        P("dp", "fsdp"),
        P(("dp", "fsdp"), None),
        P(("dp", "fsdp"), None),
        P(("dp", "fsdp")),
        P(("dp", "fsdp")),
        P("dp", "fsdp"),
        P(("dp", "fsdp")),
        P("dp", "fsdp"),
        P(("dp", "fsdp")),
    )
    out_specs = (
        P(("dp", "fsdp"), None, None),
        P(("dp", "fsdp"), None, None),
        P(("dp", "fsdp")),
        P(("dp", "fsdp")),
        P("dp", "fsdp"),
        P(("dp", "fsdp")),
        P(("dp", "fsdp")),
        P("dp", "fsdp"),
        P(("dp", "fsdp")),
        P("dp", "fsdp"),
        P("dp", "fsdp"),
        P(("dp", "fsdp"), None),
        P(("dp", "fsdp"), None),
        P(("dp", "fsdp")),
        P(("dp", "fsdp")),
        P("dp", "fsdp"),
        P(("dp", "fsdp")),
        P("dp", "fsdp"),
        P(("dp", "fsdp")),
        P(("dp", "fsdp"), None),
    )
    return jax.shard_map(local, mesh=mesh, in_specs=in_specs, out_specs=out_specs, check_vma=False)
```

profile of v0, /device:TPU:0, one launch (start us, length us, event | category | flops | bytes accessed | tf_op | source)
XLA Modules:
  0.0 1107.0 jit_solution(7771014690373540836)
XLA Ops:
  49.8 21.8 %all-gather = bf16[16,32,12]{1,2,0:T(8,128)(2,1)S(1)} all-gather(bf16[1,32,12]{1,2,0:T(8,128)(2,1)S(1)} %copy.151), channel_id=1, replica_groups=mesh['dp'=16,'fsdp'=2] {'dp'}, dimensions={0}, use_global_device_ids=true | all-gather | bytes 13056 | tf_op jit(solution)/shard_map/all_gather | solution.py:132
  76.4 17.3 %all-gather.1 = bf16[16,32,12]{1,2,0:T(8,128)(2,1)S(1)} all-gather(bf16[1,32,12]{1,2,0:T(8,128)(2,1)S(1)} %copy.153), channel_id=1, replica_groups=mesh['dp'=16,'fsdp'=2] {'dp'}, dimensions={0}, use_global_device_ids=true | all-gather | bytes 13056 | tf_op jit(solution)/shard_map/all_gather | solution.py:131
  109.9 59.4 %all-reduce.38 = (bf16[768]{0:T(1024)(128)(2,1)}, bf16[768]{0:T(1024)(128)(2,1)}, bf16[768]{0:T(1024)(128)(2,1)S(1)}, bf16[768]{0:T(1024)(128)(2,1)S(1)}, bf16[7...) all-reduce(bf16[768]{0:T(1024)(128)(2,1)S(1)} %dynamic-update-slice, ...), channel_id=1, replica_groups=mesh['dp'=16,'fsdp'=2] {'dp'}, use_global_device_ids=true, to_apply=%add.8 | all-reduce | flops 8448 | bytes 33792
  183.8 11.7 %cholesky.104 = f32[128,128]{1,0:T(8,128)S(1)} custom-call(f32[128,128]{1,0:T(8,128)S(1)} %cholesky.266), custom_call_target="Cholesky" | custom-call | tf_op jit(solution)/shard_map/jit(cholesky)/cholesky | solution.py:71
  208.8 11.7 %cholesky.217 = f32[128,128]{1,0:T(8,128)S(1)} custom-call(f32[128,128]{1,0:T(8,128)S(1)} %cholesky.270), custom_call_target="Cholesky" | custom-call | tf_op jit(solution)/shard_map/jit(cholesky)/cholesky | solution.py:71
  232.6 12.1 %cholesky.238 = f32[128,128]{1,0:T(8,128)S(1)} custom-call(f32[128,128]{1,0:T(8,128)S(1)} %cholesky.275), custom_call_target="Cholesky" | custom-call | tf_op jit(solution)/shard_map/jit(cholesky)/cholesky | solution.py:71
  256.6 11.7 %cholesky.255 = f32[128,128]{1,0:T(8,128)S(1)} custom-call(f32[128,128]{1,0:T(8,128)S(1)} %convolution_subtract_fusion.8), custom_call_target="Cholesky" | custom-call | tf_op jit(solution)/shard_map/jit(cholesky)/cholesky | solution.py:71
  272.7 14.0 %while.1 = (s32[]{:T(128)}, f32[512,512]{1,0:T(8,128)}, s32[4,2]{0,1:T(2,128)S(1)}, f32[4,128,128]{2,1,0:T(8,128)}, s32[]{:T(128)}) while((s32[]{:T(128)}, f32[512,512]{1,0:T(8,128)}, s32[4,2]{0,1:T(2,128)S(1)}, f32[4,128,128]{2,1,0:T(8,128)}, s32[]{:T(128)}) %tuple.63), condition=%wide.while_cond, body=%wide.while_body.sunk | while | flops 2 | bytes 132205 | solution.py:72
  286.7 40.3 %custom-call.37 = f32[4,128,128]{1,2,0:T(8,128)S(1)} custom-call(f32[4,128,128]{2,1,0:T(8,128)} %get-tuple-element.27), custom_call_target="InvertDiagBlocksLowerTriangular" | custom-call | tf_op jit(solution)/shard_map/jit(_cho_solve)/triangular_solve | solution.py:72
  442.4 10.7 fusion.4
  546.0 30.9 %reduce-scatter.35.cloned.1.call-done = bf16[32,12]{1,0:T(8,128)(2,1)} async-done(((bf16[512,12]{1,0:T(8,128)(2,1)}), bf16[32,12]{1,0:T(8,128)(2,1)}) %reduce-scatter.35.cloned.1.call-update) | async-done | bytes 784 | tf_op jit(solution)/shard_map/reduce_scatter | solution.py:186
  576.9 60.6 %reduce-scatter.29.cloned.1.call-done = bf16[48,768]{1,0:T(8,128)(2,1)} async-done(((bf16[768,768]{1,0:T(8,128)(2,1)}), bf16[48,768]{1,0:T(8,128)(2,1)}) %reduce-scatter.29.cloned.1.call-update) | async-done | bytes 73744 | tf_op jit(solution)/shard_map/reduce_scatter | solution.py:186
  640.1 57.9 %reduce-scatter.33.cloned.1.call-done = bf16[48,768]{1,0:T(8,128)(2,1)} async-done(((bf16[768,768]{1,0:T(8,128)(2,1)}), bf16[48,768]{1,0:T(8,128)(2,1)}) %reduce-scatter.33.cloned.1.call-update) | async-done | bytes 73744 | tf_op jit(solution)/shard_map/reduce_scatter | solution.py:186
  701.5 57.2 %reduce-scatter.31.cloned.1.call-done = bf16[48,768]{1,0:T(8,128)(2,1)} async-done(((bf16[768,768]{1,0:T(8,128)(2,1)}), bf16[48,768]{1,0:T(8,128)(2,1)}) %reduce-scatter.31.cloned.1.call-update) | async-done | bytes 73744 | tf_op jit(solution)/shard_map/reduce_scatter | solution.py:186
  760.6 58.7 %all-reduce.37 = (bf16[768]{0:T(1024)(128)(2,1)S(1)}, bf16[768]{0:T(1024)(128)(2,1)S(1)}, bf16[768]{0:T(1024)(128)(2,1)S(1)}, bf16[768]{0:T(1024)(128)(2,1)S(1)}...) all-reduce(bf16[768]{0:T(1024)(128)(2,1)S(1)} %dynamic-update-slice, ...), channel_id=1, replica_groups=mesh['dp'=16,'fsdp'=2] {'dp'}, use_global_device_ids=true, to_apply=%add.18 | all-reduce | flops 9984 | bytes 39936
  819.3 10.6 reduce-scatter.27.cloned.1.call-done
  848.9 59.3 %reduce-scatter.47.cloned.1.call-done = bf16[192,768]{1,0:T(8,128)(2,1)} async-done(((bf16[3072,768]{1,0:T(8,128)(2,1)}), bf16[192,768]{1,0:T(8,128)(2,1)}) %reduce-scatter.47.cloned.1.call-update) | async-done | bytes 294928 | tf_op jit(solution)/shard_map/reduce_scatter | solution.py:186
  913.7 73.4 %reduce-scatter.43.cloned.1.call-done = bf16[48,3072]{1,0:T(8,128)(2,1)} async-done(((bf16[768,3072]{1,0:T(8,128)(2,1)}), bf16[48,3072]{1,0:T(8,128)(2,1)}) %reduce-scatter.43.cloned.1.call-update) | async-done | bytes 294928 | tf_op jit(solution)/shard_map/reduce_scatter | solution.py:186
  1011.0 12.4 %reduce-scatter.51.cloned.1.call-done = bf16[384,48]{1,0:T(8,128)(2,1)} async-done(((bf16[768,48]{1,0:T(8,128)(2,1)}), bf16[384,48]{1,0:T(8,128)(2,1)}) %reduce-scatter.51.cloned.1.call-update) | async-done | bytes 36880
  1025.0 12.0 %reduce-scatter.55.cloned.1.call-done = bf16[384,48]{1,0:T(8,128)(2,1)} async-done(((bf16[768,48]{1,0:T(8,128)(2,1)}), bf16[384,48]{1,0:T(8,128)(2,1)}) %reduce-scatter.55.cloned.1.call-update) | async-done | bytes 36880
  1038.7 12.2 %reduce-scatter.53.cloned.1.call-done = bf16[384,48]{1,0:T(8,128)(2,1)} async-done(((bf16[768,48]{1,0:T(8,128)(2,1)}), bf16[384,48]{1,0:T(8,128)(2,1)}) %reduce-scatter.53.cloned.1.call-update) | async-done | bytes 36880
  1052.5 15.8 %reduce-scatter.49.cloned.1.call-done = bf16[1152,48]{1,0:T(8,128)(2,1)} async-done(((bf16[2304,48]{1,0:T(8,128)(2,1)}), bf16[1152,48]{1,0:T(8,128)(2,1)}) %reduce-scatter.49.cloned.1.call-update) | async-done | bytes 110608
  1070.1 13.7 %reduce-scatter.57.cloned.1.call-done = bf16[384,192]{1,0:T(8,128)(2,1)} async-done(((bf16[768,192]{1,0:T(8,128)(2,1)}), bf16[384,192]{1,0:T(8,128)(2,1)}) %reduce-scatter.57.cloned.1.call-update) | async-done | bytes 147472
  1085.5 12.5 %reduce-scatter.45.cloned.1.call-done = bf16[48,1536]{1,0:T(8,128)(2,1)} async-done(((bf16[48,3072]{1,0:T(8,128)(2,1)}), bf16[48,1536]{1,0:T(8,128)(2,1)}) %reduce-scatter.45.cloned.1.call-update) | async-done | bytes 147472 | tf_op jit(solution)/shard_map/reduce_scatter | solution.py:228
  (483 shorter events, 398.1 us)
Async XLA Ops:
  7.2 321.5 %copy-start = (bf16[1,512,768]{2,1,0:T(8,128)(2,1)S(1)}, bf16[1,512,768]{2,1,0:T(8,128)(2,1)}, u32[]{:S(2)}) copy-start(bf16[1,512,768]{2,1,0:T(8,128)(2,1)} %param.26) | copy-start | bytes 2359300
  7.4 340.7 %all-gather.11.cloned.1.call-start = ((), (), s32[]{:S(2)}) async-start(), calls=%async_computation.17 | async-start | bytes 1253376 | tf_op jit(solution)/shard_map/all_gather | solution.py:130
  14.8 336.5 %all-gather.13.cloned.1.call-start = ((), (), s32[]{:S(2)}) async-start(), calls=%async_computation.18 | async-start | bytes 1253376 | tf_op jit(solution)/shard_map/all_gather | solution.py:129
  19.8 334.7 %all-gather.9.cloned.1.call-start = ((), (), s32[]{:S(2)}) async-start(), calls=%async_computation.16 | async-start | bytes 3760128 | tf_op jit(solution)/shard_map/all_gather | solution.py:124
  26.5 378.9 %all-gather.15.cloned.1.call-start = ((), (), s32[]{:S(2)}) async-start(), calls=%async_computation.19 | async-start | bytes 1253376 | tf_op jit(solution)/shard_map/all_gather | solution.py:127
  31.5 377.5 %all-gather.17.cloned.1.call-start = ((), (), s32[]{:S(2)}) async-start(), calls=%async_computation.20 | async-start | bytes 5013504 | tf_op jit(solution)/shard_map/all_gather | solution.py:135
  38.9 378.7 %all-gather.19.cloned.1.call-start = ((), (), s32[]{:S(2)}) async-start(), calls=%async_computation.21 | async-start | bytes 5013504 | tf_op jit(solution)/shard_map/all_gather | solution.py:137
  45.2 495.6 %reduce-scatter.39.cloned.1.call-start = ((), (), s32[]{:S(2)}) async-start(), calls=%async_computation.28 | async-start | bytes 139264 | tf_op jit(solution)/shard_map/reduce_scatter | solution.py:186
  466.8 110.0 %reduce-scatter.35.cloned.1.call-start = ((), (), s32[]{:S(2)}) async-start(), calls=%async_computation.26 | async-start | bytes 139264 | tf_op jit(solution)/shard_map/reduce_scatter | solution.py:186
  467.7 169.8 %reduce-scatter.29.cloned.1.call-start = ((), (), s32[]{:S(2)}) async-start(), calls=%async_computation.23 | async-start | bytes 1253376 | tf_op jit(solution)/shard_map/reduce_scatter | solution.py:186
  470.9 227.1 %reduce-scatter.33.cloned.1.call-start = ((), (), s32[]{:S(2)}) async-start(), calls=%async_computation.25 | async-start | bytes 1253376 | tf_op jit(solution)/shard_map/reduce_scatter | solution.py:186
  485.9 272.9 %reduce-scatter.31.cloned.1.call-start = ((), (), s32[]{:S(2)}) async-start(), calls=%async_computation.24 | async-start | bytes 1253376 | tf_op jit(solution)/shard_map/reduce_scatter | solution.py:186
  502.7 327.2 %reduce-scatter.27.cloned.1.call-start = ((), (), s32[]{:S(2)}) async-start(), calls=%async_computation.22 | async-start | bytes 3760128 | tf_op jit(solution)/shard_map/reduce_scatter | solution.py:186
  519.8 388.5 %reduce-scatter.47.cloned.1.call-start = ((), (), s32[]{:S(2)}) async-start(), calls=%async_computation.32 | async-start | bytes 5013504 | tf_op jit(solution)/shard_map/reduce_scatter | solution.py:186
  528.5 458.6 %reduce-scatter.43.cloned.1.call-start = ((), (), s32[]{:S(2)}) async-start(), calls=%async_computation.30 | async-start | bytes 5013504 | tf_op jit(solution)/shard_map/reduce_scatter | solution.py:186
  536.6 461.4 %reduce-scatter.41.cloned.1.call-start = ((), (), s32[]{:S(2)}) async-start(), calls=%async_computation.29 | async-start | bytes 12288 | tf_op jit(solution)/shard_map/reduce_scatter | solution.py:219
  540.8 468.9 %reduce-scatter.37.cloned.1.call-start = ((), (), s32[]{:S(2)}) async-start(), calls=%async_computation.27 | async-start | bytes 12288 | tf_op jit(solution)/shard_map/reduce_scatter | solution.py:216
  545.9 286.0 %copy-start.15 = (f32[512,768]{1,0:T(8,128)}, f32[512,768]{1,0:T(8,128)S(1)}, u32[]{:S(2)}) copy-start(f32[512,768]{1,0:T(8,128)S(1)} %get-tuple-element.130) | copy-start | bytes 4718596
  576.9 446.5 %reduce-scatter.51.cloned.1.call-start = ((), (), s32[]{:S(2)}) async-start(), calls=%async_computation.34 | async-start | bytes 294912
  639.3 397.8 %reduce-scatter.55.cloned.1.call-start = ((), (), s32[]{:S(2)}) async-start(), calls=%async_computation.36 | async-start | bytes 294912
  699.7 351.1 %reduce-scatter.53.cloned.1.call-start = ((), (), s32[]{:S(2)}) async-start(), calls=%async_computation.35 | async-start | bytes 294912
  760.5 307.8 %reduce-scatter.49.cloned.1.call-start = ((), (), s32[]{:S(2)}) async-start(), calls=%async_computation.33 | async-start | bytes 884736
  831.9 251.8 %reduce-scatter.57.cloned.1.call-start = ((), (), s32[]{:S(2)}) async-start(), calls=%async_computation.37 | async-start | bytes 589824
  910.2 187.9 %reduce-scatter.45.cloned.1.call-start = ((), (), s32[]{:S(2)}) async-start(), calls=%async_computation.31 | async-start | bytes 442368 | tf_op jit(solution)/shard_map/reduce_scatter | solution.py:228
  (92 other events, 3441.3 us)
Sparse Core Ops, SparseCore 0:
  14.9 38.7 all-gather.10
  56.0 37.3 all-gather.12
  95.7 46.0 all-gather.8
  144.0 37.4 all-gather.14
  183.6 52.4 all-gather.16
  238.3 52.5 all-gather.18
  466.9 52.2 reduce-scatter.38
  522.7 54.1 reduce-scatter.34
  580.5 57.0 reduce-scatter.28
  641.0 56.9 reduce-scatter.32
  701.6 57.0 reduce-scatter.30
  762.5 67.3 reduce-scatter.26
  833.8 74.4 reduce-scatter.46
  912.4 74.6 reduce-scatter.42
  989.1 8.7 reduce-scatter.40
  1000.0 9.7 reduce-scatter.36
  1012.4 10.9 reduce-scatter.50
  1026.0 10.9 reduce-scatter.54
  1039.8 10.9 reduce-scatter.52
  1052.9 15.2 reduce-scatter.48
  1070.6 13.1 reduce-scatter.56
  1085.9 12.0 reduce-scatter.44
where the time goes:
time: 1110 us
  waiting for transfers between devices  447 us (40%)
  blocking collectives  214 us (19%)
  matrix products  198 us (18%)
  other arithmetic  170 us (15%)
  local copies, waits for them, and re-layouts  52.7 us (5%)
  between operations  25 us (2%)
    reduce_scatter x8, waiting for transfers between devices, spread_grads(): lax.psum_scatter(for_sending(totals), 'dp', scatter_dimension=0, tiled=True)  350 us
    unnamed x4, blocking collectives  129 us
    another operation x15, other arithmetic, memory_coeffs(): factor = jnp.linalg.cholesky(gram_matrix)  79.5 us
    unnamed x27, waiting for transfers between devices  66.4 us
    another operation x3, other arithmetic, memory_coeffs(): return jax.scipy.linalg.cho_solve((factor, True), right_side)  41.4 us
    unnamed x251, local copies, waits for them, and re-layouts  26.7 us
  transfers between devices with their start and end apart: 22, of which 15 were waited for; matrix products, arithmetic and copies ran while one was open for 33% of the time, Pallas kernels for 0%

commit v1 on v0

--- a/solution.py
+++ b/solution.py
@@ -1,6 +1,10 @@
+import functools
+
 import jax
 import jax.numpy as jnp
 from jax import lax
+from jax.experimental import pallas as pl
+from jax.experimental.pallas import tpu as pltpu
 from jax.sharding import PartitionSpec as P
 
 H = 12
@@ -17,14 +21,6 @@
 norm_epsilon = 1e-05
 spread_scale = 0.25
 masked_fill = -1e30
-
-
-def for_sending(value):
-
-    def short(part):
-        return part.astype(jnp.bfloat16) if part.dtype == jnp.float32 else part
-
-    return jax.tree.map(short, value)
 
 
 def layer_norm(values, norm_gain, norm_shift):
@@ -98,146 +94,208 @@
     return (allowed, reading.astype(jnp.float32))
 
 
-def collect_first(shards):
-    within = (
-        lax.all_gather(shards[0], "fsdp", axis=0, tiled=True),
-        lax.all_gather(shards[1], "fsdp", axis=0, tiled=True),
-        lax.all_gather(shards[2], "fsdp", axis=1, tiled=True),
-        lax.all_gather(shards[3], "fsdp", axis=0, tiled=True),
-        lax.all_gather(shards[4], "fsdp", axis=0, tiled=True),
-        lax.all_gather(shards[5], "fsdp", axis=1, tiled=True),
-        lax.all_gather(shards[6], "fsdp", axis=0, tiled=True),
-        lax.all_gather(shards[7], "fsdp", axis=1, tiled=True),
-        lax.all_gather(shards[8], "fsdp", axis=1, tiled=True),
-        lax.all_gather(shards[9], "fsdp", axis=0, tiled=True),
-        lax.all_gather(shards[10], "fsdp", axis=0, tiled=True),
-        lax.all_gather(shards[11], "fsdp", axis=0, tiled=True),
-        lax.all_gather(shards[12], "fsdp", axis=0, tiled=True),
-        lax.all_gather(shards[13], "fsdp", axis=1, tiled=True),
-        lax.all_gather(shards[14], "fsdp", axis=0, tiled=True),
-        lax.all_gather(shards[15], "fsdp", axis=1, tiled=True),
-        lax.all_gather(shards[16], "fsdp", axis=0, tiled=True),
-    )
-    return (
-        lax.all_gather(within[0], "dp", axis=0, tiled=True),
-        lax.all_gather(within[1], "dp", axis=0, tiled=True),
-        lax.all_gather(within[2], "dp", axis=0, tiled=True),
-        lax.all_gather(within[3], "dp", axis=0, tiled=True),
-        lax.all_gather(within[4], "dp", axis=0, tiled=True),
-        lax.all_gather(within[5], "dp", axis=0, tiled=True),
-        lax.all_gather(within[6], "dp", axis=0, tiled=True),
-        lax.all_gather(within[7], "dp", axis=0, tiled=True),
-        lax.all_gather(within[8], "dp", axis=0, tiled=True),
-        lax.all_gather(within[9], "dp", axis=0, tiled=True),
-        lax.all_gather(within[10], "dp", axis=0, tiled=True),
-        lax.all_gather(within[11], "dp", axis=0, tiled=True),
-        lax.all_gather(within[12], "dp", axis=0, tiled=True),
-        lax.all_gather(within[13], "dp", axis=0, tiled=True),
-        lax.all_gather(within[14], "dp", axis=0, tiled=True),
-        lax.all_gather(within[15], "dp", axis=0, tiled=True),
-        lax.all_gather(within[16], "dp", axis=0, tiled=True),
-    )
-
-
-def collect_again(shards):
-    within = (
-        lax.all_gather(shards[0], "fsdp", axis=0, tiled=True),
-        lax.all_gather(shards[1], "fsdp", axis=0, tiled=True),
-        lax.all_gather(shards[2], "fsdp", axis=1, tiled=True),
-        lax.all_gather(shards[3], "fsdp", axis=0, tiled=True),
-        lax.all_gather(shards[4], "fsdp", axis=0, tiled=True),
-        lax.all_gather(shards[5], "fsdp", axis=1, tiled=True),
-        lax.all_gather(shards[6], "fsdp", axis=0, tiled=True),
-        lax.all_gather(shards[7], "fsdp", axis=1, tiled=True),
-        lax.all_gather(shards[8], "fsdp", axis=1, tiled=True),
-        lax.all_gather(shards[9], "fsdp", axis=0, tiled=True),
-        lax.all_gather(shards[10], "fsdp", axis=0, tiled=True),
-        lax.all_gather(shards[11], "fsdp", axis=0, tiled=True),
-        lax.all_gather(shards[12], "fsdp", axis=0, tiled=True),
-        lax.all_gather(shards[13], "fsdp", axis=1, tiled=True),
-        lax.all_gather(shards[14], "fsdp", axis=0, tiled=True),
-        lax.all_gather(shards[15], "fsdp", axis=1, tiled=True),
-        lax.all_gather(shards[16], "fsdp", axis=0, tiled=True),
-    )
-    return (
-        lax.all_gather(within[0], "dp", axis=0, tiled=True),
-        lax.all_gather(within[1], "dp", axis=0, tiled=True),
-        lax.all_gather(within[2], "dp", axis=0, tiled=True),
-        lax.all_gather(within[3], "dp", axis=0, tiled=True),
-        lax.all_gather(within[4], "dp", axis=0, tiled=True),
-        lax.all_gather(within[5], "dp", axis=0, tiled=True),
-        lax.all_gather(within[6], "dp", axis=0, tiled=True),
-        lax.all_gather(within[7], "dp", axis=0, tiled=True),
-        lax.all_gather(within[8], "dp", axis=0, tiled=True),
-        lax.all_gather(within[9], "dp", axis=0, tiled=True),
-        lax.all_gather(within[10], "dp", axis=0, tiled=True),
-        lax.all_gather(within[11], "dp", axis=0, tiled=True),
-        lax.all_gather(within[12], "dp", axis=0, tiled=True),
-        lax.all_gather(within[13], "dp", axis=0, tiled=True),
-        lax.all_gather(within[14], "dp", axis=0, tiled=True),
-        lax.all_gather(within[15], "dp", axis=0, tiled=True),
-        lax.all_gather(within[16], "dp", axis=0, tiled=True),
-    )
-
-
-def spread_grads(totals):
-    partial_sums = jax.tree.map(
-        lambda part: part.astype(jnp.float32),
-        lax.psum_scatter(for_sending(totals), "dp", scatter_dimension=0, tiled=True),
-    )
-    return (
-        lax.psum_scatter(
-            partial_sums[0].astype(jnp.bfloat16), "fsdp", scatter_dimension=0, tiled=True
-        ).astype(jnp.float32),
-        lax.psum_scatter(
-            partial_sums[1].astype(jnp.bfloat16), "fsdp", scatter_dimension=0, tiled=True
-        ).astype(jnp.float32),
-        lax.psum_scatter(
-            partial_sums[2].astype(jnp.bfloat16), "fsdp", scatter_dimension=1, tiled=True
-        ).astype(jnp.float32),
-        lax.psum_scatter(
-            partial_sums[3].astype(jnp.bfloat16), "fsdp", scatter_dimension=0, tiled=True
-        ).astype(jnp.float32),
-        lax.psum_scatter(
-            partial_sums[4].astype(jnp.bfloat16), "fsdp", scatter_dimension=0, tiled=True
-        ).astype(jnp.float32),
-        lax.psum_scatter(
-            partial_sums[5].astype(jnp.bfloat16), "fsdp", scatter_dimension=1, tiled=True
-        ).astype(jnp.float32),
-        lax.psum_scatter(
-            partial_sums[6].astype(jnp.bfloat16), "fsdp", scatter_dimension=0, tiled=True
-        ).astype(jnp.float32),
-        lax.psum_scatter(
-            partial_sums[7].astype(jnp.bfloat16), "fsdp", scatter_dimension=1, tiled=True
-        ).astype(jnp.float32),
-        lax.psum_scatter(
-            partial_sums[8].astype(jnp.bfloat16), "fsdp", scatter_dimension=1, tiled=True
-        ).astype(jnp.float32),
-        lax.psum_scatter(
-            partial_sums[9].astype(jnp.bfloat16), "fsdp", scatter_dimension=0, tiled=True
-        ).astype(jnp.float32),
-        lax.psum_scatter(
-            partial_sums[10].astype(jnp.bfloat16), "fsdp", scatter_dimension=0, tiled=True
-        ).astype(jnp.float32),
-        lax.psum_scatter(
-            partial_sums[11].astype(jnp.bfloat16), "fsdp", scatter_dimension=0, tiled=True
-        ).astype(jnp.float32),
-        lax.psum_scatter(
-            partial_sums[12].astype(jnp.bfloat16), "fsdp", scatter_dimension=0, tiled=True
-        ).astype(jnp.float32),
-        lax.psum_scatter(
-            partial_sums[13].astype(jnp.bfloat16), "fsdp", scatter_dimension=1, tiled=True
-        ).astype(jnp.float32),
-        lax.psum_scatter(
-            partial_sums[14].astype(jnp.bfloat16), "fsdp", scatter_dimension=0, tiled=True
-        ).astype(jnp.float32),
-        lax.psum_scatter(
-            partial_sums[15].astype(jnp.bfloat16), "fsdp", scatter_dimension=1, tiled=True
-        ).astype(jnp.float32),
-        lax.psum_scatter(
-            partial_sums[16].astype(jnp.bfloat16), "fsdp", scatter_dimension=0, tiled=True
-        ).astype(jnp.float32),
-    )
+BOTH = ("dp", "fsdp")
+SMALL_COLUMNS = 128
+
+
+def hypercube(mesh_sizes):
+    return mesh_sizes == (16, 2)
+
+
+def place_of():
+    dp = lax.axis_index("dp")
+    return dp // 4, (dp // 2) % 2, dp % 2, lax.axis_index("fsdp")
+
+
+def hop(value, z=0, x=0, core=0, f=0):
+    pairs = []
+    for dp in range(16):
+        for side in range(2):
+            other = (((dp // 4) ^ z) * 4) + ((((dp // 2) % 2) ^ x) * 2) + ((dp % 2) ^ core)
+            pairs.append((dp * 2 + side, other * 2 + (side ^ f)))
+    return lax.ppermute(value, BOTH, pairs)
+
+
+def gather_hops(block, x_first):
+    quad = jnp.stack([block] + [hop(block, z=k) for k in (1, 2, 3)])
+    first, second = (dict(x=1), dict(f=1)) if x_first else (dict(f=1), dict(x=1))
+    near = hop(quad, **first)
+    mine = [quad, near, hop(quad, **second), hop(near, **second)]
+    return mine + [hop(part, core=1) for part in mine]
+
+
+def block_offsets(x_first):
+    for array in range(8):
+        core, first, second = array // 4, array % 2, (array // 2) % 2
+        x, f = (first, second) if x_first else (second, first)
+        for z in range(4):
+            yield array, z, z, x, core, f
+
+
+def join_blocks(place, proj_parts, mem_parts, late_parts):
+    rows, proj_columns = proj_parts[0].shape[1:]
+    square = late_parts.shape[-1] // 9
+    width = 16 * rows
+
+    def kernel(place_ref, *refs):
+        proj_refs, mem_refs, late_ref = refs[:8], refs[8:16], refs[16]
+        proj, keys, values, small, out, up, down, sem = refs[17:]
+        copies = []
+
+        def move(source, target):
+            copy = pltpu.make_async_copy(source, target, sem)
+            copy.start()
+            copies.append(copy)
+
+        for x_first, parts in ((True, proj_refs), (False, mem_refs)):
+            for array, index, z, x, core, f in block_offsets(x_first):
+                dp = (place_ref[0] ^ z) * 4 + (place_ref[1] ^ x) * 2 + (place_ref[2] ^ core)
+                side = place_ref[3] ^ f
+                at = pl.ds(pl.multiple_of(dp * rows, 16), rows)
+                source = parts[array].at[index]
+                if x_first:
+                    move(source, proj.at[at, pl.ds(pl.multiple_of(side * proj_columns, 128), proj_columns)])
+                else:
+                    across = pl.ds(pl.multiple_of(side * square, 128), square)
+                    move(source.at[:, pl.ds(0, square)], keys.at[at, across])
+                    move(source.at[:, pl.ds(square, square)], values.at[at, across])
+                    move(source.at[:, pl.ds(2 * square, SMALL_COLUMNS)], small.at[dp * 2 + side])
+        for dp in range(16):
+            for side in range(2):
+                source = late_ref.at[dp * 2 + side]
+                at = pl.ds(dp * rows, rows)
+                move(source.at[:, pl.ds(0, square)], out.at[at, pl.ds(side * square, square)])
+                move(source.at[:, pl.ds(square, 4 * square)], up.at[at, pl.ds(side * 4 * square, 4 * square)])
+                for q in range(4):
+                    move(
+                        source.at[:, pl.ds((5 + q) * square, square)],
+                        down.at[pl.ds(dp * 4 * rows + q * rows, rows), pl.ds(side * square, square)],
+                    )
+        for copy in copies:
+            copy.wait()
+
+    shapes = [
+        (width, 2 * proj_columns),
+        (width, width),
+        (width, width),
+        (32, rows, SMALL_COLUMNS),
+        (width, width),
+        (width, 4 * width),
+        (4 * width, width),
+    ]
+    return pl.pallas_call(
+        kernel,
+        out_shape=[jax.ShapeDtypeStruct(shape, jnp.bfloat16) for shape in shapes],
+        in_specs=[pl.BlockSpec(memory_space=pltpu.SMEM)] + [pl.BlockSpec(memory_space=pl.ANY)] * 17,
+        out_specs=[pl.BlockSpec(memory_space=pl.ANY)] * 7,
+        scratch_shapes=[pltpu.SemaphoreType.DMA],
+        cost_estimate=pl.CostEstimate(flops=0, bytes_accessed=33_000_000, transcendentals=0),
+    )(place, *proj_parts, *mem_parts, late_parts)
+
+
+def collect_hops(shards):
+    rows, square = shards[5].shape
+    vectors = [shards[k] for k in VECTORS]
+    small = jnp.concatenate([v.reshape(-1) for v in vectors + [shards[k] for k in TABLES]])
+    small = jnp.pad(small, (0, rows * SMALL_COLUMNS - small.shape[0])).reshape(rows, SMALL_COLUMNS)
+    late = jnp.concatenate(
+        [shards[5], shards[13]] + [shards[15][q * rows : (q + 1) * rows] for q in range(4)], axis=1
+    )
+    late_parts = lax.all_gather(late, BOTH, axis=0)
+    mem_parts = gather_hops(jnp.concatenate([shards[7], shards[8], small], axis=1), False)
+    proj_parts = gather_hops(shards[2], True)
+    place = jnp.stack(place_of()).astype(jnp.int32)
+    proj, keys, values, small, out, up, down = join_blocks(place, proj_parts, mem_parts, late_parts)
+    small = small.reshape(32, rows * SMALL_COLUMNS)
+    found = {2: proj, 5: out, 7: keys, 8: values, 13: up, 15: down}
+    at = 0
+    for k in VECTORS + TABLES:
+        size = shards[k].size
+        found[k] = small[:, at : at + size].reshape((-1,) + shards[k].shape[1:])
+        at += size
+    return tuple(found[k] for k in range(17))
+
+
+VECTORS = [0, 1, 3, 4, 6, 11, 12, 16, 14]
+TABLES = [9, 10]
+COLUMN_SPLIT = (2, 5, 7, 8, 13, 15)
+
+
+def collect(shards, mesh_sizes):
+    if hypercube(mesh_sizes):
+        return collect_hops(shards)
+
+    def whole(k, shard):
+        near = lax.all_gather(shard, "fsdp", axis=1 if k in COLUMN_SPLIT else 0, tiled=True)
+        return lax.all_gather(near, "dp", axis=0, tiled=True)
+
+    return tuple(whole(k, shard) for k, shard in enumerate(shards))
+
+
+def scatter_hops(total, x_first):
+    z, x, core, f = place_of()
+    rows, columns = total.shape
+    value = total.reshape(4, 2, 2, rows // 16, columns)
+
+    def pick(array, axis, index):
+        return lax.dynamic_index_in_dim(array, index, axis, keepdims=False)
+
+    def pick_columns(array, index):
+        return lax.dynamic_slice_in_dim(array, index * (columns // 2), columns // 2, array.ndim - 1)
+
+    def plus(a, b):
+        return (a.astype(jnp.float32) + b.astype(jnp.float32)).astype(jnp.bfloat16)
+
+    kept, got = pick(value, 2, core), hop(pick(value, 2, 1 - core), core=1)
+
+    def by_x(kept, got):
+        sent = plus(pick(kept, 1, 1 - x), pick(got, 1, 1 - x))
+        return plus(pick(kept, 1, x), pick(got, 1, x)), hop(sent, x=1)
+
+    def by_f(kept, got):
+        sent = plus(pick_columns(kept, 1 - f), pick_columns(got, 1 - f))
+        return plus(pick_columns(kept, f), pick_columns(got, f)), hop(sent, f=1)
+
+    for step in (by_x, by_f) if x_first else (by_f, by_x):
+        kept, got = step(kept, got)
+    result = pick(kept, 0, z).astype(jnp.float32) + pick(got, 0, z).astype(jnp.float32)
+    for k in (1, 2, 3):
+        result = result + hop(plus(pick(kept, 0, z ^ k), pick(got, 0, z ^ k)), z=k).astype(jnp.float32)
+    return result
+
+
+def spread_hops(grads, shards):
+    bf = jnp.bfloat16
+    rows, square = shards[5].shape
+    summed = {13: scatter_hops(grads[13].astype(bf), True), 15: scatter_hops(grads[15].astype(bf), False)}
+    halves = [grads[k].astype(bf).reshape(-1, 2, square) for k in (5, 7, 8)]
+    middle = scatter_hops(jnp.concatenate(halves, axis=2).reshape(-1, 6 * square), False)
+    for n, k in enumerate((5, 7, 8)):
+        summed[k] = middle[:, n * square : (n + 1) * square]
+    small = jnp.concatenate([grads[k].astype(bf).reshape(32, -1) for k in VECTORS + TABLES], axis=1)
+    small = jnp.pad(small, ((0, 0), (0, rows * SMALL_COLUMNS - small.shape[1])))
+    small = small.reshape(16, 2, rows, SMALL_COLUMNS).transpose(0, 2, 1, 3).reshape(-1, 2, SMALL_COLUMNS)
+    proj = grads[2].astype(bf).reshape(small.shape[0], 2, -1)
+    last = jnp.concatenate([proj, small], axis=2)
+    last = scatter_hops(last.reshape(last.shape[0], -1), True)
+    summed[2] = last[:, : proj.shape[2]]
+    small, at = last[:, proj.shape[2] :].reshape(-1), 0
+    for k in VECTORS + TABLES:
+        summed[k] = small[at : at + shards[k].size].reshape(shards[k].shape)
+        at += shards[k].size
+    return tuple(summed[k] for k in range(17))
+
+
+def spread(grads, shards, mesh_sizes):
+    if hypercube(mesh_sizes):
+        return spread_hops(grads, shards)
+
+    def part(k, grad):
+        near = lax.psum_scatter(grad.astype(jnp.bfloat16), "dp", scatter_dimension=0, tiled=True)
+        axis = 1 if k in COLUMN_SPLIT else 0
+        return lax.psum_scatter(near, "fsdp", scatter_dimension=axis, tiled=True).astype(jnp.float32)
+
+    return tuple(part(k, grad) for k, grad in enumerate(grads))
 
 
 def short_scores(queries, key_rows, allowed):
@@ -519,6 +577,7 @@
 
 
 def local(
+    mesh_sizes,
     tokens,
     context,
     past_coeffs,
@@ -563,7 +622,7 @@
         down_weight,
         down_bias,
     )
-    weights = collect_first(shards)
+    weights = collect(shards, mesh_sizes)
     points = jax.vmap(sample_points)(histogram)
     seg_rows = tokens.shape[1]
     segment_index = 0
@@ -577,11 +636,10 @@
     results = [result.astype(jnp.bfloat16)]
     states = [kept_state]
     settings = [(coeff_low, allowed, reading)]
-    back_weights = collect_again(shards)
     segment_index = 0
     coeff_low, allowed, reading = settings[segment_index]
     grad_inputs, grads = backward_segment(
-        cotangent[segment_index], coeff_low, allowed, reading, states[segment_index], back_weights
+        cotangent[segment_index], coeff_low, allowed, reading, states[segment_index], weights
     )
     input_grads = [grad_inputs]
     (
@@ -602,7 +660,7 @@
         grad_up_bias,
         grad_down_weight,
         grad_down_bias,
-    ) = spread_grads(grads)
+    ) = spread(grads, shards, mesh_sizes)
     return (
         jnp.stack(results),
         jnp.stack(input_grads),
@@ -676,4 +734,5 @@
         P(("dp", "fsdp")),
         P(("dp", "fsdp"), None),
     )
-    return jax.shard_map(local, mesh=mesh, in_specs=in_specs, out_specs=out_specs, check_vma=False)
+    sizes = (mesh.shape["dp"], mesh.shape["fsdp"])
+    return jax.shard_map(functools.partial(local, sizes), mesh=mesh, in_specs=in_specs, out_specs=out_specs, check_vma=False)

time: 1110 us -> 1150 us (1.036)
  Pallas kernels: 0 us -> 514 us
  waiting for transfers between devices: 447 us -> 91.3 us
  blocking collectives: 214 us -> 0 us
  local copies, waits for them, and re-layouts: 52.7 us -> 106 us
  starting transfers between devices: 1.16 us -> 43.5 us
    pallas_call x0 -> x1, Pallas kernels: none -> 514 us  [join_blocks(): pl.pallas_call(kernel, out_shape=[jax.ShapeDtypeStruct(shape, jnp.bfloat1...]
    reduce_scatter x11 -> x0, waiting for transfers between devices: 380 us -> none  [the longest x8 350 us: spread_grads(): lax.psum_scatter(for_sending(totals), 'dp', scatter_dimension=0, tiled=True)]
    unnamed x4 -> x0, blocking collectives: 129 us -> none
    ppermute x0 -> x44, waiting for transfers between devices: none -> 91.2 us  [hop(): return lax.ppermute(value, BOTH, pairs)]
    all_gather x10 -> x0, blocking collectives: 85.4 us -> none  [the longest x1 21.8 us: collect_first(): lax.all_gather(within[10], 'dp', axis=0, tiled=True)]
    unnamed x27 -> x1, waiting for transfers between devices: 66.4 us -> 0.02 us
    ppermute x0 -> x44, starting transfers between devices: none -> 43.4 us  [hop(): return lax.ppermute(value, BOTH, pairs)]
    reshape x0 -> x19, local copies, waits for them, and re-layouts: none -> 28.3 us  [the longest x3 13.1 us: spread_hops(): halves = [grads[k].astype(bf).reshape(-1, 2, square) for k in (5, 7, 8)]]
  transfers between devices with their start and end apart: 22 -> 45, of which waited for: 15 -> 18; matrix products, arithmetic and copies ran while one was open for 33% -> 22% of each run, Pallas kernels for 0% -> 0%
where the time goes in v1:
time: 1150 us; the launch traced here: 1140 us
  Pallas kernels  514 us (45%)
  matrix products  187 us (16%)
  other arithmetic  175 us (15%)
  local copies, waits for them, and re-layouts  106 us (9%)
  waiting for transfers between devices  91.3 us (8%)
  starting transfers between devices  43.5 us (4%)
  between operations  19.5 us (2%)
    pallas_call x1, Pallas kernels, join_blocks(): pl.pallas_call(kernel, out_shape=[jax.ShapeDtypeStruct(shape, jnp.bfloat1...  514 us
    ppermute x44, waiting for transfers between devices, hop(): return lax.ppermute(value, BOTH, pairs)  91.2 us
    another operation x15, other arithmetic, memory_coeffs(): factor = jnp.linalg.cholesky(gram_matrix)  79.5 us
    ppermute x44, starting transfers between devices, hop(): return lax.ppermute(value, BOTH, pairs)  43.4 us
    another operation x3, other arithmetic, memory_coeffs(): return jax.scipy.linalg.cho_solve((factor, True), right_side)  40.5 us
  transfers between devices with their start and end apart: 45, of which 18 were waited for; matrix products, arithmetic and copies ran while one was open for 22% of the time, Pallas kernels for 0%

profile of v1, /device:TPU:0, one launch (start us, length us, event | category | flops | bytes accessed | tf_op | source)
XLA Modules:
  0.0 1136.9 jit_solution(2615267629768892235)
XLA Ops:
  43.4 11.9 %cholesky.104 = f32[128,128]{1,0:T(8,128)S(1)} custom-call(f32[128,128]{1,0:T(8,128)S(1)} %cholesky.266), custom_call_target="Cholesky" | custom-call | tf_op jit(solution)/shard_map/jit(cholesky)/cholesky | solution.py:67
  55.3 9.8 custom-call.34
  67.8 11.7 %cholesky.217 = f32[128,128]{1,0:T(8,128)S(1)} custom-call(f32[128,128]{1,0:T(8,128)S(1)} %cholesky.270), custom_call_target="Cholesky" | custom-call | tf_op jit(solution)/shard_map/jit(cholesky)/cholesky | solution.py:67
  79.5 9.8 custom-call.35
  90.9 12.1 %cholesky.238 = f32[128,128]{1,0:T(8,128)S(1)} custom-call(f32[128,128]{1,0:T(8,128)S(1)} %cholesky.275), custom_call_target="Cholesky" | custom-call | tf_op jit(solution)/shard_map/jit(cholesky)/cholesky | solution.py:67
  103.0 9.8 custom-call.36
  114.3 11.7 %cholesky.255 = f32[128,128]{1,0:T(8,128)S(1)} custom-call(f32[128,128]{1,0:T(8,128)S(1)} %convolution_subtract_fusion.8), custom_call_target="Cholesky" | custom-call | tf_op jit(solution)/shard_map/jit(cholesky)/cholesky | solution.py:67
  131.3 10.5 while.1
  141.8 40.3 %custom-call.37 = f32[4,128,128]{1,2,0:T(8,128)S(1)} custom-call(f32[4,128,128]{2,1,0:T(8,128)} %get-tuple-element.41), custom_call_target="InvertDiagBlocksLowerTriangular" | custom-call | tf_op jit(solution)/shard_map/jit(_cho_solve)/triangular_solve | solution.py:68
  187.1 8.6 fusion.53
  227.0 7.9 collective-permute-done.4.refs_2_
  234.9 8.7 collective-permute-done.5.refs_3_
  250.4 514.0 %shard_map.383 = (bf16[768,2304]{1,0:T(8,128)(2,1)}, bf16[768,768]{1,0:T(8,128)(2,1)}, bf16[768,768]{1,0:T(8,128)(2,1)}, bf16[32,48,128]{2,1,0:T(8,128)(2,1)}, b...) custom-call(s32[4]{0:T(128)} %pad_add_fusion.place_ref, ...), custom_call_target="tpu_custom_call" | custom-call | bytes 33000000 | tf_op jit(solution)/shard_map/pallas_call | solution.py:186
  864.1 9.6 multiply_reduce_fusion
  885.4 10.9 fusion.4
  915.7 9.4 fusion.12
  925.1 9.2 fusion.10
  960.5 9.1 reshape_reshape.7
  982.0 7.9 reshape.981
  997.5 9.7 reshape_reshape.6
  1009.3 9.1 fusion.98
  1026.5 16.7 %collective-permute-done.27 = bf16[4,2,48,1152]{3,2,1,0:T(8,128)(2,1)S(1)} collective-permute-done((bf16[4,2,48,1152]{3,2,1,0:T(8,128)(2,1)S(1)}, bf16[4,2,48,1152]{3,2,1,0:T(8,128)(2,1)S(1)}, u32[]{:S(2)}, u32[]{:S(2)}) %collective-permute-start.27) | collective-permute-done | bytes 884768 | tf_op jit(solution)/shard_map/ppermute | solution.py:116
  1072.9 12.1 %collective-permute-done.22 = bf16[4,48,1280]{2,1,0:T(8,128)(2,1)S(1)} collective-permute-done((bf16[4,48,1280]{2,1,0:T(8,128)(2,1)S(1)}, bf16[4,48,1280]{2,1,0:T(8,128)(2,1)S(1)}, u32[]{:S(2)}, u32[]{:S(2)}) %collective-permute-start.22) | collective-permute-done | bytes 491552 | tf_op jit(solution)/shard_map/ppermute | solution.py:116
  1113.8 11.1 collective-permute-done.42
  (502 shorter events, 346.3 us)
Async XLA Ops:
  7.2 242.3 %all-gather.3.cloned.1.call-start = ((), (), s32[]{:S(2)}) async-start(), calls=%async_computation | async-start | bytes 10948608 | tf_op jit(solution)/shard_map/all_gather | solution.py:204
  12.9 191.1 %collective-permute-start = (bf16[48,1152]{1,0:T(8,128)(2,1)}, bf16[48,1152]{1,0:T(8,128)(2,1)S(1)}, u32[]{:S(2)}, u32[]{:S(2)}) collective-permute-start(bf16[48,1152]{1,0:T(8,128)(2,1)} %param.33), channel_id=1, source_target_pairs={{0,8},{1,9},{2,10},{3,11},{4,12},{5,13},{6,14},{7,15},{8,0},{9,1},... | collective-permute-start | bytes 331784 | tf_op jit(solution)/shard_map/ppermute | solution.py:116
  16.0 189.0 %collective-permute-start.2 = (bf16[48,1152]{1,0:T(8,128)(2,1)}, bf16[48,1152]{1,0:T(8,128)(2,1)S(1)}, u32[]{:S(2)}, u32[]{:S(2)}) collective-permute-start(bf16[48,1152]{1,0:T(8,128)(2,1)} %param.33), channel_id=1, source_target_pairs={{0,24},{1,25},{2,26},{3,27},{4,28},{5,29},{6,30},{7,31},{8,16},{9,... | collective-permute-start | bytes 331784 | tf_op jit(solution)/shard_map/ppermute | solution.py:116
  18.5 186.5 %collective-permute-start.1 = (bf16[48,1152]{1,0:T(8,128)(2,1)}, bf16[48,1152]{1,0:T(8,128)(2,1)}, u32[]{:S(2)}, u32[]{:S(2)}) collective-permute-start(bf16[48,1152]{1,0:T(8,128)(2,1)} %param.33), channel_id=1, source_target_pairs={{0,16},{1,17},{2,18},{3,19},{4,20},{5,21},{6,22},{7,23},{8,24},{9,... | collective-permute-start | bytes 331784 | tf_op jit(solution)/shard_map/ppermute | solution.py:116
  27.7 180.6 %collective-permute-start.11 = (bf16[48,896]{1,0:T(8,128)(2,1)}, bf16[48,896]{1,0:T(8,128)(2,1)}, u32[]{:S(2)}, u32[]{:S(2)}) collective-permute-start(bf16[48,896]{1,0:T(8,128)(2,1)} %get-tuple-element.120), channel_id=1, source_target_pairs={{0,16},{1,17},{2,18},{3,19},{4,20},{5,21},{6,22},{7,23},{8,24},{9,... | collective-permute-start | bytes 258056 | tf_op jit(solution)/shard_map/ppermute | solution.py:116
  30.5 177.8 %collective-permute-start.10 = (bf16[48,896]{1,0:T(8,128)(2,1)}, bf16[48,896]{1,0:T(8,128)(2,1)}, u32[]{:S(2)}, u32[]{:S(2)}) collective-permute-start(bf16[48,896]{1,0:T(8,128)(2,1)} %get-tuple-element.120), channel_id=1, source_target_pairs={{0,8},{1,9},{2,10},{3,11},{4,12},{5,13},{6,14},{7,15},{8,0},{9,1},... | collective-permute-start | bytes 258056 | tf_op jit(solution)/shard_map/ppermute | solution.py:116
  216.0 18.9 %collective-permute-start.4 = (bf16[4,48,1152]{2,1,0:T(8,128)(2,1)S(1)}, bf16[4,48,1152]{2,1,0:T(8,128)(2,1)}, u32[]{:S(2)}, u32[]{:S(2)}) collective-permute-start(bf16[4,48,1152]{2,1,0:T(8,128)(2,1)S(1)} %pad_maximum_fusion.4.refs_0_), channel_id=1, source_target_pairs={{0,1},{1,0},{2,3},{3,2},{4,5},{5,4},{6,7},{7,6},{8,9},{9,8},{10,11... | collective-permute-start | bytes 1327112 | tf_op jit(solution)/shard_map/ppermute | solution.py:116
  218.7 25.0 %collective-permute-start.5 = (bf16[4,48,1152]{2,1,0:T(8,128)(2,1)}, bf16[4,48,1152]{2,1,0:T(8,128)(2,1)}, u32[]{:S(2)}, u32[]{:S(2)}) collective-permute-start(bf16[4,48,1152]{2,1,0:T(8,128)(2,1)} %collective-permute-done.3.refs_1_), channel_id=1, source_target_pairs={{0,1},{1,0},{2,3},{3,2},{4,5},{5,4},{6,7},{7,6},{8,9},{9,8},{10,11... | collective-permute-start | bytes 1327112 | tf_op jit(solution)/shard_map/ppermute | solution.py:116
  224.8 21.3 %collective-permute-start.18 = (bf16[4,48,896]{2,1,0:T(8,128)(2,1)}, bf16[4,48,896]{2,1,0:T(8,128)(2,1)S(1)}, u32[]{:S(2)}, u32[]{:S(2)}) collective-permute-start(bf16[4,48,896]{2,1,0:T(8,128)(2,1)} %collective-permute-done.14.refs_10_), channel_id=1, source_target_pairs={{0,2},{1,3},{2,0},{3,1},{4,6},{5,7},{6,4},{7,5},{8,10},{9,11},{10,... | collective-permute-start | bytes 1032200 | tf_op jit(solution)/shard_map/ppermute | solution.py:116
  225.4 21.1 %collective-permute-start.15 = (bf16[4,48,896]{2,1,0:T(8,128)(2,1)}, bf16[4,48,896]{2,1,0:T(8,128)(2,1)}, u32[]{:S(2)}, u32[]{:S(2)}) collective-permute-start(bf16[4,48,896]{2,1,0:T(8,128)(2,1)} %collective-permute-done.13.refs_9_), channel_id=1, source_target_pairs={{0,4},{1,5},{2,6},{3,7},{4,0},{5,1},{6,2},{7,3},{8,12},{9,13},{10,... | collective-permute-start | bytes 1032200 | tf_op jit(solution)/shard_map/ppermute | solution.py:116
  226.7 22.8 %collective-permute-start.7 = (bf16[4,48,1152]{2,1,0:T(8,128)(2,1)}, bf16[4,48,1152]{2,1,0:T(8,128)(2,1)S(1)}, u32[]{:S(2)}, u32[]{:S(2)}) collective-permute-start(bf16[4,48,1152]{2,1,0:T(8,128)(2,1)} %collective-permute-done.3.refs_1_), channel_id=1, source_target_pairs={{0,2},{1,3},{2,0},{3,1},{4,6},{5,7},{6,4},{7,5},{8,10},{9,11},{10,... | collective-permute-start | bytes 1327112 | tf_op jit(solution)/shard_map/ppermute | solution.py:116
  972.5 45.9 %collective-permute-start.26 = (bf16[4,2,48,2304]{3,2,1,0:T(8,128)(2,1)}, bf16[4,2,48,2304]{3,2,1,0:T(8,128)(2,1)}, u32[]{:S(2)}, u32[]{:S(2)}) collective-permute-start(bf16[4,2,48,2304]{3,2,1,0:T(8,128)(2,1)} %dynamic-slice_bitcast_fusion.1), channel_id=1, source_target_pairs={{0,2},{1,3},{2,0},{3,1},{4,6},{5,7},{6,4},{7,5},{8,10},{9,11},{10,... | collective-permute-start | bytes 5308424 | tf_op jit(solution)/shard_map/ppermute | solution.py:116
  979.6 64.5 %collective-permute-start.38 = (bf16[4,2,192,768]{3,2,1,0:T(8,128)(2,1)}, bf16[4,2,192,768]{3,2,1,0:T(8,128)(2,1)}, u32[]{:S(2)}, u32[]{:S(2)}) collective-permute-start(bf16[4,2,192,768]{3,2,1,0:T(8,128)(2,1)} %dynamic-slice_bitcast_fusion), channel_id=1, source_target_pairs={{0,2},{1,3},{2,0},{3,1},{4,6},{5,7},{6,4},{7,5},{8,10},{9,11},{10,... | collective-permute-start | bytes 7077896 | tf_op jit(solution)/shard_map/ppermute | solution.py:116
  979.7 69.0 %collective-permute-start.32 = (bf16[4,2,48,3072]{3,2,0,1:T(8,128)(2,1)}, bf16[4,2,48,3072]{3,2,0,1:T(8,128)(2,1)}, u32[]{:S(2)}, u32[]{:S(2)}) collective-permute-start(bf16[4,2,48,3072]{3,2,0,1:T(8,128)(2,1)} %copy_bitcast_fusion), channel_id=1, source_target_pairs={{0,2},{1,3},{2,0},{3,1},{4,6},{5,7},{6,4},{7,5},{8,10},{9,11},{10,... | collective-permute-start | bytes 7077896 | tf_op jit(solution)/shard_map/ppermute | solution.py:116
  1021.1 22.1 %collective-permute-start.27 = (bf16[4,2,48,1152]{3,2,1,0:T(8,128)(2,1)S(1)}, bf16[4,2,48,1152]{3,2,1,0:T(8,128)(2,1)S(1)}, u32[]{:S(2)}, u32[]{:S(2)}) collective-permute-start(bf16[4,2,48,1152]{3,2,1,0:T(8,128)(2,1)S(1)} %get-tuple-element.78), channel_id=1, source_target_pairs={{0,1},{1,0},{2,3},{3,2},{4,5},{5,4},{6,7},{7,6},{8,9},{9,8},{10,11... | collective-permute-start | bytes 2654216 | tf_op jit(solution)/shard_map/ppermute | solution.py:116
  1025.9 36.1 %collective-permute-start.21 = (bf16[4,48,2560]{2,1,0:T(8,128)(2,1)S(1)}, bf16[4,48,2560]{2,1,0:T(8,128)(2,1)S(1)}, u32[]{:S(2)}, u32[]{:S(2)}) collective-permute-start(bf16[4,48,2560]{2,1,0:T(8,128)(2,1)S(1)} %get-tuple-element.76), channel_id=1, source_target_pairs={{0,4},{1,5},{2,6},{3,7},{4,0},{5,1},{6,2},{7,3},{8,12},{9,13},{10,... | collective-permute-start | bytes 2949128 | tf_op jit(solution)/shard_map/ppermute | solution.py:116
  1043.4 16.6 %collective-permute-start.28 = (bf16[4,48,1152]{2,1,0:T(8,128)(2,1)S(1)}, bf16[4,48,1152]{2,1,0:T(8,128)(2,1)S(1)}, u32[]{:S(2)}, u32[]{:S(2)}) collective-permute-start(bf16[4,48,1152]{2,1,0:T(8,128)(2,1)S(1)} %get-tuple-element.89), channel_id=1, source_target_pairs={{0,4},{1,5},{2,6},{3,7},{4,0},{5,1},{6,2},{7,3},{8,12},{9,13},{10,... | collective-permute-start | bytes 1327112 | tf_op jit(solution)/shard_map/ppermute | solution.py:116
  1047.1 41.5 %collective-permute-start.39 = (bf16[4,2,192,384]{3,2,1,0:T(8,128)(2,1)S(1)}, bf16[4,2,192,384]{3,2,1,0:T(8,128)(2,1)S(1)}, u32[]{:S(2)}, u32[]{:S(2)}) collective-permute-start(bf16[4,2,192,384]{3,2,1,0:T(8,128)(2,1)S(1)} %get-tuple-element.72), channel_id=1, source_target_pairs={{0,1},{1,0},{2,3},{3,2},{4,5},{5,4},{6,7},{7,6},{8,9},{9,8},{10,11... | collective-permute-start | bytes 3538952 | tf_op jit(solution)/shard_map/ppermute | solution.py:116
  1051.3 40.0 %collective-permute-start.33 = (bf16[4,48,3072]{2,1,0:T(8,128)(2,1)S(1)}, bf16[4,48,3072]{2,1,0:T(8,128)(2,1)S(1)}, u32[]{:S(2)}, u32[]{:S(2)}) collective-permute-start(bf16[4,48,3072]{2,1,0:T(8,128)(2,1)S(1)} %get-tuple-element.74), channel_id=1, source_target_pairs={{0,4},{1,5},{2,6},{3,7},{4,0},{5,1},{6,2},{7,3},{8,12},{9,13},{10,... | collective-permute-start | bytes 3538952 | tf_op jit(solution)/shard_map/ppermute | solution.py:116
  1066.8 18.2 %collective-permute-start.22 = (bf16[4,48,1280]{2,1,0:T(8,128)(2,1)S(1)}, bf16[4,48,1280]{2,1,0:T(8,128)(2,1)S(1)}, u32[]{:S(2)}, u32[]{:S(2)}) collective-permute-start(bf16[4,48,1280]{2,1,0:T(8,128)(2,1)S(1)} %get-tuple-element.87), channel_id=1, source_target_pairs={{0,1},{1,0},{2,3},{3,2},{4,5},{5,4},{6,7},{7,6},{8,9},{9,8},{10,11... | collective-permute-start | bytes 1474568 | tf_op jit(solution)/shard_map/ppermute | solution.py:116
  1105.7 19.1 %collective-permute-start.42 = (bf16[192,384]{1,0:T(8,128)(2,1)S(1)}, bf16[192,384]{1,0:T(8,128)(2,1)S(1)}, u32[]{:S(2)}, u32[]{:S(2)}) collective-permute-start(bf16[192,384]{1,0:T(8,128)(2,1)S(1)} %get-tuple-element.92), channel_id=1, source_target_pairs={{0,16},{1,17},{2,18},{3,19},{4,20},{5,21},{6,22},{7,23},{8,24},{9,... | collective-permute-start | bytes 442376 | tf_op jit(solution)/shard_map/ppermute | solution.py:116
  1106.6 19.0 %collective-permute-start.35 = (bf16[48,1536]{1,0:T(8,128)(2,1)S(1)}, bf16[48,1536]{1,0:T(8,128)(2,1)S(1)}, u32[]{:S(2)}, u32[]{:S(2)}) collective-permute-start(bf16[48,1536]{1,0:T(8,128)(2,1)S(1)} %get-tuple-element.93), channel_id=1, source_target_pairs={{0,8},{1,9},{2,10},{3,11},{4,12},{5,13},{6,14},{7,15},{8,0},{9,1},... | collective-permute-start | bytes 442376 | tf_op jit(solution)/shard_map/ppermute | solution.py:116
  1108.8 16.8 %collective-permute-start.37 = (bf16[48,1536]{1,0:T(8,128)(2,1)S(1)}, bf16[48,1536]{1,0:T(8,128)(2,1)S(1)}, u32[]{:S(2)}, u32[]{:S(2)}) collective-permute-start(bf16[48,1536]{1,0:T(8,128)(2,1)S(1)} %get-tuple-element.94), channel_id=1, source_target_pairs={{0,24},{1,25},{2,26},{3,27},{4,28},{5,29},{6,30},{7,31},{8,16},{9,... | collective-permute-start | bytes 442376 | tf_op jit(solution)/shard_map/ppermute | solution.py:116
  1112.8 16.2 %collective-permute-start.36 = (bf16[48,1536]{1,0:T(8,128)(2,1)S(1)}, bf16[48,1536]{1,0:T(8,128)(2,1)S(1)}, u32[]{:S(2)}, u32[]{:S(2)}) collective-permute-start(bf16[48,1536]{1,0:T(8,128)(2,1)S(1)} %get-tuple-element.95), channel_id=1, source_target_pairs={{0,16},{1,17},{2,18},{3,19},{4,20},{5,21},{6,22},{7,23},{8,24},{9,... | collective-permute-start | bytes 442376 | tf_op jit(solution)/shard_map/ppermute | solution.py:116
  (117 other events, 2407.0 us)
Sparse Core Ops, SparseCore 0:
  13.0 93.0 all-gather.2
